TPU v7x, 512 devices: a whole 4x4x16 slice. The times are simulated.
512 devices in a mesh: band: 8 (over x, core), pw: 64 (over z, y).
Axes of the slice: x: 4, y: 4, z: 16, core: 2. Of those that a mesh axis runs over, the one named last changes fastest.
Arguments:
- orbital_coefficients: float32 [8, 2, 128, 128, 128], P('band', None, 'pw'), may hold values from -6 to 6
- sphere_halfwidth: int32 [128, 128], P('pw'), may hold values from -1 to 63, as said below
- occupation: float32 [8], P('band'), may hold values from 0.5 to 2
- local_potential: float32 [256, 256, 256], P(None, 'pw'), may hold values from -6 to 6
- stencil_corner: int32 [64, 64, 128], P('pw'), may hold values from 0 to 262143, as said below
- stencil_weight: float32 [8, 64, 64, 128], P(None, 'pw'), may hold values from -3 to 3
- point_count: int32 [64, 64], P('pw'), may hold values from 0 to 128, as said below
Outputs:
- local_action: float32 [8, 2, 128, 128, 128], P('band', None, 'pw')
- fit_potential: float32 [64, 64, 128], P('pw')
Inputs may be any that keep to these rules, and one draw needn't show every extreme that they name: `sphere_halfwidth`: in every draw the kept columns form one sphere centred at frequency zero that reaches the cube's faces; -1 marks an empty column. `stencil_corner`: each corner is x * 4 + y times 256 plus z, with x and z in 0 to 255 and y in 0 to 3. `point_count`: in every draw some tile has all 128 slots live from every source, and every source has some block with all 128 slots live.
All inputs are finite; a program needn't handle non-finite values.
Results may differ from a plain program's by a relative error of at most 0.0003.
Values sent between devices are 32-bit elements; how exact they have to be, the bound alone decides.
A program may use at most 64 MiB of HBM per device.

v0:
```python
import math
import jax
import jax.numpy as jnp
from jax import lax
from jax.sharding import PartitionSpec as P

hartree_scale = 200.0
exact_mode = lax.Precision.HIGHEST


def shifted(value, axis, steps):
    count = lax.axis_size(axis)
    pairs = [(source, (source + steps) % count) for source in range(count)]
    return lax.ppermute(value, axis, pairs)


def phases(frequency, grid_size):
    position = jnp.arange(grid_size, dtype=jnp.int32)
    product = jnp.remainder(frequency[:, None] * position[None, :], grid_size)
    angle = product.astype(jnp.float32) * (2.0 * math.pi / grid_size)
    return (jnp.cos(angle), jnp.sin(angle))


def inverse_table(frequency, grid_size):
    cosine, sine = phases(frequency, grid_size)
    from_real = jnp.stack([cosine, sine], axis=1)
    from_imag = jnp.stack([-sine, cosine], axis=1)
    return jnp.stack([from_real, from_imag], axis=0)


def forward_table(frequency, grid_size):
    cosine, sine = phases(frequency, grid_size)
    from_real = jnp.stack([cosine.T, -sine.T], axis=1)
    from_imag = jnp.stack([sine.T, cosine.T], axis=1)
    return jnp.stack([from_real, from_imag], axis=0)


def transform(operand, matrix, target_axis, component_axis):
    result = lax.dot_general(
        operand,
        matrix,
        (((component_axis, target_axis), (0, 1)), ((), ())),
        precision=exact_mode,
        preferred_element_type=jnp.float32,
    )
    dimensions = operand.ndim
    return jnp.moveaxis(result, (dimensions - 2, dimensions - 1), (component_axis, target_axis))


def kernel_values(start_x, count_x, start_y, count_y, grid_size):

    def signed(start, count):
        frequency = start + jnp.arange(count, dtype=jnp.int32)
        return jnp.where(frequency < grid_size // 2, frequency, frequency - grid_size)

    along_x = signed(start_x, count_x)
    along_y = signed(start_y, count_y)
    along_z = signed(0, grid_size)
    square = along_x[:, None, None] ** 2 + along_y[None, :, None] ** 2 + along_z[None, None, :] ** 2
    return jnp.where(square > 0, hartree_scale / jnp.maximum(square, 1).astype(jnp.float32), 0.0)


def body(
    orbital_coefficients,
    sphere_halfwidth,
    occupation,
    local_potential,
    stencil_corner,
    stencil_weight,
    point_count,
):
    cube_size = orbital_coefficients.shape[3]
    grid_size = local_potential.shape[0]
    slab_depth = local_potential.shape[1]
    slot_count = stencil_corner.shape[2]
    cube_freq = jnp.arange(cube_size, dtype=jnp.int32) - cube_size // 2
    sphere_mask = (jnp.abs(cube_freq)[None, None, :] <= sphere_halfwidth[:, :, None]).astype(
        jnp.float32
    )
    scale_in = float(cube_size) ** (-1.5)
    scale_out = float(cube_size) ** 1.5 / float(grid_size) ** 3
    inverse_cube = inverse_table(cube_freq, grid_size)
    forward_cube = forward_table(cube_freq, grid_size)
    coefficient = orbital_coefficients * (sphere_mask * scale_in)[None, None]
    partial_section = transform(coefficient, inverse_cube, 4, 1)
    partial_section = transform(partial_section, inverse_cube, 3, 1)
    orbital = transform(
        lax.all_to_all(partial_section, "pw", split_axis=3, concat_axis=2, tiled=True),
        inverse_cube,
        2,
        1,
    )
    partial_density = jnp.sum(
        occupation[:, None, None, None] * (orbital[:, 0] ** 2 + orbital[:, 1] ** 2), axis=0
    )
    product = orbital * local_potential[None, None]
    forward_section = transform(product, forward_cube, 2, 1)
    pencil = lax.all_to_all(forward_section, "pw", split_axis=2, concat_axis=3, tiled=True)
    pencil = transform(pencil, forward_cube, 3, 1)
    spectrum_cube = transform(pencil, forward_cube, 4, 1)
    local_action = spectrum_cube * (sphere_mask * scale_out)[None, None]
    grid_freq = jnp.arange(grid_size, dtype=jnp.int32)
    forward_grid = forward_table(grid_freq, grid_size)
    inverse_grid = inverse_table(grid_freq, grid_size)
    pw_count = lax.axis_size("pw")
    band_count = lax.axis_size("band")
    x_block = grid_size // pw_count
    x_start = lax.axis_index("pw") * x_block
    inverse_norm = 1.0 / float(grid_size) ** 3
    y_block = grid_size // band_count
    y_start = lax.axis_index("band") * y_block
    density_part = lax.psum_scatter(partial_density, "band", scatter_dimension=2, tiled=True)
    spectrum = transform(density_part[None], forward_grid[0:1], 1, 0)
    spectrum = lax.all_to_all(spectrum, "pw", split_axis=1, concat_axis=2, tiled=True)
    spectrum = transform(spectrum, forward_grid, 2, 0)
    spectrum = lax.all_to_all(spectrum, "band", split_axis=2, concat_axis=3, tiled=True)
    spectrum = transform(spectrum, forward_grid, 3, 0)
    spectrum = spectrum * kernel_values(x_start, x_block, y_start, y_block, grid_size)[None]
    spectrum = transform(spectrum, inverse_grid, 3, 0)
    spectrum = lax.all_to_all(spectrum, "band", split_axis=3, concat_axis=2, tiled=True)
    spectrum = transform(spectrum, inverse_grid, 2, 0)
    spectrum = lax.all_to_all(spectrum, "pw", split_axis=2, concat_axis=1, tiled=True)
    hartree_part = transform(spectrum, inverse_grid[:, :, 0:1], 1, 0)[0] * inverse_norm
    hartree = lax.all_gather(hartree_part, "band", axis=2, tiled=True)
    upper_plane = shifted(hartree[:, 0:1, :], "pw", -1)
    extended = jnp.concatenate([hartree, upper_plane], axis=1)
    flattened = extended.reshape(-1)
    plane_cells = slab_depth * grid_size
    request = lax.all_to_all(stencil_corner, "pw", split_axis=1, concat_axis=0, tiled=True)
    coord_x = request // plane_cells
    coord_y = request // grid_size % slab_depth
    coord_z = request % grid_size
    gathered = []
    for corner in range(8):
        step_x = corner // 4
        step_y = corner // 2 % 2
        step_z = corner % 2
        cell_index = (
            (coord_x + step_x) % grid_size * (slab_depth + 1) + coord_y + step_y
        ) * grid_size + (coord_z + step_z) % grid_size
        gathered.append(flattened[cell_index])
    stacked = jnp.stack(gathered, axis=0)
    sampled = lax.all_to_all(stacked, "pw", split_axis=1, concat_axis=2, tiled=True)
    summed = jnp.sum(stencil_weight * sampled, axis=0)
    live_slot = jnp.arange(slot_count, dtype=jnp.int32)[None, None, :] < point_count[:, :, None]
    fit_potential = jnp.where(live_slot, summed, 0.0)
    return (local_action, fit_potential)


def solution(mesh):
    placed = (
        P("band", None, "pw", None, None),
        P("pw", None),
        P("band"),
        P(None, "pw", None),
        P("pw", None, None),
        P(None, "pw", None, None),
        P("pw", None),
    )
    return jax.shard_map(
        body,
        mesh=mesh,
        in_specs=placed,
        out_specs=(P("band", None, "pw", None, None), P("pw", None, None)),
        check_vma=False,
    )
```

profile of v0, /device:TPU:8, one launch (start us, length us, event | category | flops | bytes accessed | tf_op | source)
XLA Modules:
  0.0 736.5 jit_solution(2443056056476492475)
XLA Ops:
  11.6 18.7 %all-to-all-start = ((f32[1,2,2,256,256]{4,1,2,0,3:T(2,128)}), f32[1,2,2,256,256]{4,1,2,0,3:T(2,128)S(1)}, u32[]{:S(2)}, u32[]{:S(2)}) async-start(f32[1,2,2,256,256]{4,1,2,0,3:T(2,128)} %copy.52), calls=%async_computation | async-start | bytes 2097152 | tf_op jit(solution)/shard_map/all_to_all | solution.py:88
  31.1 54.5 %all-to-all-done = f32[1,2,2,256,256]{4,1,2,0,3:T(2,128)S(1)} async-done(((f32[1,2,2,256,256]{4,1,2,0,3:T(2,128)}), f32[1,2,2,256,256]{4,1,2,0,3:T(2,128)S(1)}, u32[]{:S(2)}, u32[]{:S(2)}) %all-to-all-start) | async-done | bytes 1048608 | tf_op jit(solution)/shard_map/all_to_all | solution.py:88
  86.4 1.9 convolution_bitcast_fusion
  91.4 29.4 %reduce-scatter.2.cloned.1.call-done = f32[256,4,32]{0,2,1:T(8,128)} async-done(((f32[256,4,256]{0,2,1:T(8,128)}), f32[256,4,32]{0,2,1:T(8,128)}) %reduce-scatter.2.cloned.1.call-update) | async-done | bytes 131088 | tf_op jit(solution)/shard_map/reduce_scatter | solution.py:112
  120.7 2.0 fusion.33
  125.6 16.2 %all-to-all-start.2 = ((f32[64,1,1024]{2,1,0:T(1,128)}), f32[64,1,1024]{2,1,0:T(1,128)}, u32[]{:S(2)}, u32[]{:S(2)}) async-start(f32[64,1,1024]{2,1,0:T(1,128)} %reshape.1541), calls=%async_computation.3 | async-start | bytes 524288 | tf_op jit(solution)/shard_map/all_to_all | solution.py:114
  145.5 15.2 %all-to-all-done.2 = f32[64,1,1024]{2,1,0:T(1,128)} async-done(((f32[64,1,1024]{2,1,0:T(1,128)}), f32[64,1,1024]{2,1,0:T(1,128)}, u32[]{:S(2)}, u32[]{:S(2)}) %all-to-all-start.2) | async-done | bytes 262176 | tf_op jit(solution)/shard_map/all_to_all | solution.py:114
  161.2 2.2 reduce.1
  167.6 2.0 convolution_bitcast_fusion.8
  170.8 3.0 reshape.1543
  173.8 4.5 all-to-all-start.3
  179.2 6.9 all-to-all-done.3
  186.0 2.2 reduce.2
  188.2 1.9 reshape.1544
  190.1 2.8 copy.151
  192.9 1.5 all_to_all.105
  194.5 1.9 fusion.9
  198.4 2.3 reshape.1545
  200.7 10.6 %all_to_all.126 = f32[8,1,8192]{2,1,0:T(1,128)} all-to-all(f32[8,1,8192]{2,1,0:T(1,128)S(1)} %reshape.1545), channel_id=1, replica_groups=mesh['band'=8,'pw'=64] {'band'}, dimensions={0} | all-to-all | bytes 524288 | tf_op jit(solution)/shard_map/all_to_all | solution.py:120
  211.3 6.1 all-to-all-start.6
  217.5 2.2 reduce.3
  219.7 1.9 reshape.1546
  221.6 2.8 copy.150
  224.4 1.5 reshape.1535
  227.4 1.6 copy.76
  229.0 1.8 reshape.1547
  231.0 14.9 %all-to-all-start.5 = ((f32[64,1,1024]{2,1,0:T(1,128)}), f32[64,1,1024]{2,1,0:T(1,128)S(1)}, u32[]{:S(2)}, u32[]{:S(2)}) async-start(f32[64,1,1024]{2,1,0:T(1,128)} %reshape.1547), calls=%async_computation.6 | async-start | bytes 524288 | tf_op jit(solution)/shard_map/all_to_all | solution.py:122
  245.9 1.6 copy.56
  248.8 2.8 fusion.3
  251.6 2.3 copy.58
  253.8 12.9 %all-to-all-done.5 = f32[64,1,1024]{2,1,0:T(1,128)S(1)} async-done(((f32[64,1,1024]{2,1,0:T(1,128)}), f32[64,1,1024]{2,1,0:T(1,128)S(1)}, u32[]{:S(2)}, u32[]{:S(2)}) %all-to-all-start.5) | async-done | bytes 262176 | tf_op jit(solution)/shard_map/all_to_all | solution.py:122
  266.7 6.2 all-to-all-start.1
  276.9 2.4 fusion.11
  279.3 30.2 %all-gather.3.cloned.1.call-done = f32[1,256,4,256]{1,3,2,0:T(8,128)} async-done(((f32[1,256,4,32]{1,3,2,0:T(8,128)}), f32[1,256,4,256]{1,3,2,0:T(8,128)}) %all-gather.3.cloned.1.call-update) | async-done | bytes 1048592 | tf_op jit(solution)/shard_map/all_gather | solution.py:124
  310.5 2.4 collective-permute-start
  314.4 1.5 fusion.94
  315.9 6.3 collective-permute-done
  324.9 45.7 %gather_fusion.7 = f32[8192]{0:T(1024)S(1)} fusion(f32[327680]{0:T(1024)S(1)} %reshape.1420, s32[8192]{0:T(1024)} %get-tuple-element.8), kind=kCustom, calls=%fused_computation.7 | custom fusion | bytes 98304 | tf_op jit(solution)/shard_map/gather | solution.py:141
  370.6 45.5 %gather_fusion.6 = f32[8192]{0:T(1024)S(1)} fusion(f32[327680]{0:T(1024)S(1)} %reshape.1420, s32[8192]{0:T(1024)S(1)} %copy-done.18), kind=kCustom, calls=%fused_computation.6 | custom fusion | bytes 98304 | tf_op jit(solution)/shard_map/gather | solution.py:141
  416.2 45.5 %gather_fusion.5 = f32[8192]{0:T(1024)S(1)} fusion(f32[327680]{0:T(1024)S(1)} %reshape.1420, s32[8192]{0:T(1024)S(1)} %copy-done.17), kind=kCustom, calls=%fused_computation.5 | custom fusion | bytes 98304 | tf_op jit(solution)/shard_map/gather | solution.py:141
  461.7 45.5 %gather_fusion.4 = f32[8192]{0:T(1024)S(1)} fusion(f32[327680]{0:T(1024)S(1)} %reshape.1420, s32[8192]{0:T(1024)S(1)} %copy-done.16), kind=kCustom, calls=%fused_computation.4 | custom fusion | bytes 98304 | tf_op jit(solution)/shard_map/gather | solution.py:141
  507.3 45.5 %gather_fusion.3 = f32[8192]{0:T(1024)S(1)} fusion(f32[327680]{0:T(1024)S(1)} %reshape.1420, s32[8192]{0:T(1024)S(1)} %copy-done.12), kind=kCustom, calls=%fused_computation.3 | custom fusion | bytes 98304 | tf_op jit(solution)/shard_map/gather | solution.py:141
  552.9 45.5 %gather_fusion.2 = f32[8192]{0:T(1024)S(1)} fusion(f32[327680]{0:T(1024)S(1)} %reshape.1420, s32[8192]{0:T(1024)S(1)} %copy-done.15), kind=kCustom, calls=%fused_computation.2 | custom fusion | bytes 98304 | tf_op jit(solution)/shard_map/gather | solution.py:141
  598.4 45.5 %gather_fusion.1 = f32[8192]{0:T(1024)S(1)} fusion(f32[327680]{0:T(1024)S(1)} %reshape.1420, s32[8192]{0:T(1024)S(1)} %copy-done.14), kind=kCustom, calls=%fused_computation.1 | custom fusion | bytes 98304 | tf_op jit(solution)/shard_map/gather | solution.py:141
  644.0 45.5 %gather_fusion = f32[8192]{0:T(1024)S(1)} fusion(f32[327680]{0:T(1024)S(1)} %reshape.1420, s32[8192]{0:T(1024)S(1)} %copy-done.13), kind=kCustom, calls=%fused_computation | custom fusion | bytes 98304 | tf_op jit(solution)/shard_map/gather | solution.py:141
  690.6 16.6 %all-to-all-start.7 = ((f32[8,64,1,128]{3,0,2,1:T(8,128)}), f32[8,64,1,128]{3,0,2,1:T(8,128)S(1)}, u32[]{:S(2)}, u32[]{:S(2)}) async-start(f32[8,64,1,128]{3,0,2,1:T(8,128)} %stack.131), calls=%async_computation.8 | async-start | bytes 524288 | tf_op jit(solution)/shard_map/all_to_all | solution.py:143
  709.7 1.8 convolution_bitcast_fusion.2
  713.3 15.0 %all-to-all-done.7 = f32[8,64,1,128]{3,0,2,1:T(8,128)S(1)} async-done(((f32[8,64,1,128]{3,0,2,1:T(8,128)}), f32[8,64,1,128]{3,0,2,1:T(8,128)S(1)}, u32[]{:S(2)}, u32[]{:S(2)}) %all-to-all-start.7) | async-done | bytes 262176 | tf_op jit(solution)/shard_map/all_to_all | solution.py:143
  (95 shorter events, 41.8 us)
Async XLA Ops:
  7.2 1.5 copy-start.11
  11.6 73.9 %all-to-all-start = ((f32[1,2,2,256,256]{4,1,2,0,3:T(2,128)}), f32[1,2,2,256,256]{4,1,2,0,3:T(2,128)S(1)}, u32[]{:S(2)}, u32[]{:S(2)}) async-start(f32[1,2,2,256,256]{4,1,2,0,3:T(2,128)} %copy.52), calls=%async_computation | async-start | bytes 2097152 | tf_op jit(solution)/shard_map/all_to_all | solution.py:88
  30.4 90.4 %reduce-scatter.2.cloned.1.call-start = ((), (), s32[]{:S(2)}) async-start(), calls=%async_computation.9 | async-start | bytes 1179648 | tf_op jit(solution)/shard_map/reduce_scatter | solution.py:112
  91.4 29.4 %copy-start.9 = (f32[256,1,256]{2,0,1:T(8,128)}, f32[256,1,256]{2,0,1:T(8,128)S(1)}, u32[]{:S(2)}) copy-start(f32[256,1,256]{2,0,1:T(8,128)S(1)} %fusion.57) | copy-start | bytes 786436
  125.6 35.1 %all-to-all-start.2 = ((f32[64,1,1024]{2,1,0:T(1,128)}), f32[64,1,1024]{2,1,0:T(1,128)}, u32[]{:S(2)}, u32[]{:S(2)}) async-start(f32[64,1,1024]{2,1,0:T(1,128)} %reshape.1541), calls=%async_computation.3 | async-start | bytes 524288 | tf_op jit(solution)/shard_map/all_to_all | solution.py:114
  144.0 1.3 copy-start.1
  144.1 1.4 copy-start.3
  166.4 1.2 copy-start
  173.8 12.2 %all-to-all-start.3 = ((f32[8,1,8192]{2,1,0:T(1,128)}), f32[8,1,8192]{2,1,0:T(1,128)}, u32[]{:S(2)}, u32[]{:S(2)}) async-start(f32[8,1,8192]{2,1,0:T(1,128)} %reshape.1543), calls=%async_computation.4 | async-start | bytes 524288 | tf_op jit(solution)/shard_map/all_to_all | solution.py:116
  211.3 19.6 %all-to-all-start.6 = ((s32[1,64,128]{2,0,1:T(1,128)}), s32[1,64,128]{2,0,1:T(1,128)}, u32[]{:S(2)}, u32[]{:S(2)}) async-start(s32[1,64,128]{2,0,1:T(1,128)} %bitcast.297), calls=%async_computation.7 | async-start | bytes 65536 | tf_op jit(solution)/shard_map/all_to_all | solution.py:129
  231.0 35.8 %all-to-all-start.5 = ((f32[64,1,1024]{2,1,0:T(1,128)}), f32[64,1,1024]{2,1,0:T(1,128)S(1)}, u32[]{:S(2)}, u32[]{:S(2)}) async-start(f32[64,1,1024]{2,1,0:T(1,128)} %reshape.1547), calls=%async_computation.6 | async-start | bytes 524288 | tf_op jit(solution)/shard_map/all_to_all | solution.py:122
  248.0 0.7 copy-start.5
  248.0 0.8 copy-start.7
  266.7 423.9 %all-to-all-start.1 = ((f32[1,2,128,4,256]{4,1,3,0,2:T(2,128)}), f32[1,2,128,4,256]{4,1,3,0,2:T(2,128)}, u32[]{:S(2)}, u32[]{:S(2)}) async-start(f32[1,2,128,4,256]{4,1,3,0,2:T(2,128)} %copy.58), calls=%async_computation.1 | async-start | bytes 2097152 | tf_op jit(solution)/shard_map/all_to_all | solution.py:98
  273.0 36.5 %all-gather.3.cloned.1.call-start = ((), (), s32[]{:S(2)}) async-start(), calls=%async_computation.10 | async-start | bytes 1179648 | tf_op jit(solution)/shard_map/all_gather | solution.py:124
  275.7 1.0 copy-start.2
  275.7 1.2 copy-start.4
  310.5 11.8 %collective-permute-start = (f32[256,1,256]{0,2,1:T(8,128)S(1)}, f32[256,1,256]{0,2,1:T(8,128)S(1)}, u32[]{:S(2)}, u32[]{:S(2)}) collective-permute-start(f32[256,1,256]{0,2,1:T(8,128)S(1)} %slice.36), channel_id=1, source_target_pairs={{0,63},{1,0},{2,1},{3,2},{4,3},{5,4},{6,5},{7,6},{8,7},{9,8},{10,9... | collective-permute-start | bytes 786440 | tf_op jit(solution)/shard_map/ppermute | solution.py:14
  324.9 45.7 %copy-start.18 = (s32[8192]{0:T(1024)S(1)}, s32[8192]{0:T(1024)}, u32[]{:S(2)}) copy-start(s32[8192]{0:T(1024)} %get-tuple-element.22) | copy-start | bytes 98308
  370.6 45.6 %copy-start.17 = (s32[8192]{0:T(1024)S(1)}, s32[8192]{0:T(1024)}, u32[]{:S(2)}) copy-start(s32[8192]{0:T(1024)} %get-tuple-element.23) | copy-start | bytes 98308
  416.2 45.6 %copy-start.16 = (s32[8192]{0:T(1024)S(1)}, s32[8192]{0:T(1024)}, u32[]{:S(2)}) copy-start(s32[8192]{0:T(1024)} %get-tuple-element.24) | copy-start | bytes 98308
  461.7 45.6 %copy-start.12 = (s32[8192]{0:T(1024)S(1)}, s32[8192]{0:T(1024)}, u32[]{:S(2)}) copy-start(s32[8192]{0:T(1024)} %get-tuple-element.31) | copy-start | bytes 98308
  507.3 45.6 %copy-start.15 = (s32[8192]{0:T(1024)S(1)}, s32[8192]{0:T(1024)}, u32[]{:S(2)}) copy-start(s32[8192]{0:T(1024)} %get-tuple-element.30) | copy-start | bytes 98308
  552.8 45.6 %copy-start.14 = (s32[8192]{0:T(1024)S(1)}, s32[8192]{0:T(1024)}, u32[]{:S(2)}) copy-start(s32[8192]{0:T(1024)} %get-tuple-element.29) | copy-start | bytes 98308
  598.4 45.6 %copy-start.13 = (s32[8192]{0:T(1024)S(1)}, s32[8192]{0:T(1024)}, u32[]{:S(2)}) copy-start(s32[8192]{0:T(1024)} %get-tuple-element.28) | copy-start | bytes 98308
  690.6 37.7 %all-to-all-start.7 = ((f32[8,64,1,128]{3,0,2,1:T(8,128)}), f32[8,64,1,128]{3,0,2,1:T(8,128)S(1)}, u32[]{:S(2)}, u32[]{:S(2)}) async-start(f32[8,64,1,128]{3,0,2,1:T(8,128)} %stack.131), calls=%async_computation.8 | async-start | bytes 524288 | tf_op jit(solution)/shard_map/all_to_all | solution.py:143
  708.7 1.0 copy-start.6
  708.7 1.0 copy-start.8
  711.5 16.8 %copy-start.10 = (f32[8,1,64,128]{3,2,1,0:T(8,128)S(1)}, f32[8,1,64,128]{3,2,1,0:T(8,128)}, u32[]{:S(2)}) copy-start(f32[8,1,64,128]{3,2,1,0:T(8,128)} %param.12) | copy-start | bytes 786436
  711.5 17.0 %copy-start.19 = (s32[1,64]{1,0:T(1,128)S(1)}, s32[1,64]{1,0:T(1,128)}, u32[]{:S(2)}) copy-start(s32[1,64]{1,0:T(1,128)} %param.13) | copy-start | bytes 772
Sparse Core Ops, SparseCore 0:
  89.5 31.1 reduce-scatter.1
  279.4 29.9 all-gather.2
where the time goes:
time: 746 us; the launch traced here: 737 us
  local copies, waits for them, and re-layouts  411 us (55%)
  waiting for transfers between devices  170 us (23%)
  starting transfers between devices  86.1 us (12%)
  other arithmetic  22.6 us (3%)
  matrix products  19.7 us (3%)
  between operations  15.8 us (2%)
  blocking collectives  10.6 us (1%)
    gather x8, local copies, waits for them, and re-layouts, body(): gathered.append(flattened[cell_index])  364 us
    all_to_all x1, waiting for transfers between devices, body(): lax.all_to_all(partial_section, 'pw', split_axis=3, concat_axis=2, tiled=...  54.5 us
    all_gather x1, waiting for transfers between devices, body(): hartree = lax.all_gather(hartree_part, 'band', axis=2, tiled=True)  30.2 us
    reduce_scatter x1, waiting for transfers between devices, body(): lax.psum_scatter(partial_density, 'band', scatter_dimension=2, tiled=True)  29.4 us
    dot_general x12, matrix products, transform(): lax.dot_general(operand, matrix, (((component_axis, target_axis), (0, 1))...  19.7 us
    unnamed x50, local copies, waits for them, and re-layouts  19.3 us
    all_to_all x1, starting transfers between devices, body(): lax.all_to_all(partial_section, 'pw', split_axis=3, concat_axis=2, tiled=...  18.7 us
    all_to_all x1, starting transfers between devices, body(): lax.all_to_all(stacked, 'pw', split_axis=1, concat_axis=2, tiled=True)  16.6 us
  transfers between devices with their start and end apart: 10, of which 9 were waited for; matrix products, arithmetic and copies ran while one was open for 56% of the time, Pallas kernels for 0%

commit v1 on v0

--- a/solution.py
+++ b/solution.py
@@ -6,6 +6,13 @@
 
 hartree_scale = 200.0
 exact_mode = lax.Precision.HIGHEST
+
+
+def swapped_in(x, mesh_axis, d):
+    size = lax.axis_size(mesh_axis)
+    tiles = jnp.stack([x for _ in range(size)])
+    tiles = lax.all_to_all(tiles, mesh_axis, split_axis=0, concat_axis=0)
+    return jnp.concatenate(tiles, axis=d)
 
 
 def shifted(value, axis, steps):
@@ -121,7 +128,7 @@
     spectrum = transform(spectrum, inverse_grid, 2, 0)
     spectrum = lax.all_to_all(spectrum, "pw", split_axis=2, concat_axis=1, tiled=True)
     hartree_part = transform(spectrum, inverse_grid[:, :, 0:1], 1, 0)[0] * inverse_norm
-    hartree = lax.all_gather(hartree_part, "band", axis=2, tiled=True)
+    hartree = swapped_in(hartree_part, "band", 2)
     upper_plane = shifted(hartree[:, 0:1, :], "pw", -1)
     extended = jnp.concatenate([hartree, upper_plane], axis=1)
     flattened = extended.reshape(-1)

time: 746 us -> 773 us (1.036)
  the two profiles are of different devices: /device:TPU:8 before, /device:TPU:2 now
where the time goes in v1:
time: 773 us; the launch traced here: 764 us
  local copies, waits for them, and re-layouts  414 us (54%)
  waiting for transfers between devices  176 us (23%)
  starting transfers between devices  80.7 us (10%)
  blocking collectives  38.5 us (5%)
  other arithmetic  20 us (3%)
  matrix products  19 us (2%)
  between operations  15.7 us (2%)
    gather x8, local copies, waits for them, and re-layouts, body(): gathered.append(flattened[cell_index])  364 us
    all_to_all x1, waiting for transfers between devices, body(): lax.all_to_all(partial_section, 'pw', split_axis=3, concat_axis=2, tiled=...  54.6 us
    ppermute x1, waiting for transfers between devices, shifted(): return lax.ppermute(value, axis, pairs)  40.7 us
    all_to_all x1, blocking collectives, body(): lax.all_to_all(spectrum, 'pw', split_axis=2, concat_axis=1, tiled=True)  27.7 us
    reduce_scatter x1, waiting for transfers between devices, body(): lax.psum_scatter(partial_density, 'band', scatter_dimension=2, tiled=True)  26.1 us
    unnamed x38, local copies, waits for them, and re-layouts  19.4 us
    dot_general x12, matrix products, transform(): lax.dot_general(operand, matrix, (((component_axis, target_axis), (0, 1))...  19 us
    all_to_all x1, starting transfers between devices, body(): lax.all_to_all(partial_section, 'pw', split_axis=3, concat_axis=2, tiled=...  18.7 us
  transfers between devices with their start and end apart: 9, of which 8 were waited for; matrix products, arithmetic and copies ran while one was open for 52% of the time, Pallas kernels for 0%

profile of v1, /device:TPU:2, one launch (start us, length us, event | category | flops | bytes accessed | tf_op | source)
XLA Modules:
  0.0 763.7 jit_solution(1429343301351390845)
XLA Ops:
  11.6 18.7 %all-to-all-start = ((f32[1,2,2,256,256]{4,1,2,0,3:T(2,128)}), f32[1,2,2,256,256]{4,1,2,0,3:T(2,128)S(1)}, u32[]{:S(2)}, u32[]{:S(2)}) async-start(f32[1,2,2,256,256]{4,1,2,0,3:T(2,128)} %copy.53), calls=%async_computation | async-start | bytes 2097152 | tf_op jit(solution)/shard_map/all_to_all | solution.py:95
  31.1 54.6 %all-to-all-done = f32[1,2,2,256,256]{4,1,2,0,3:T(2,128)S(1)} async-done(((f32[1,2,2,256,256]{4,1,2,0,3:T(2,128)}), f32[1,2,2,256,256]{4,1,2,0,3:T(2,128)S(1)}, u32[]{:S(2)}, u32[]{:S(2)}) %all-to-all-start) | async-done | bytes 1048608 | tf_op jit(solution)/shard_map/all_to_all | solution.py:95
  86.5 1.9 convolution_bitcast_fusion
  91.5 26.1 %reduce-scatter.2.cloned.1.call-done = f32[256,4,32]{0,2,1:T(8,128)} async-done(((f32[256,4,256]{0,2,1:T(8,128)}), f32[256,4,32]{0,2,1:T(8,128)}) %reduce-scatter.2.cloned.1.call-update) | async-done | bytes 131088 | tf_op jit(solution)/shard_map/reduce_scatter | solution.py:119
  117.6 2.0 fusion.33
  122.5 16.1 %all-to-all-start.2 = ((f32[64,1,1024]{2,1,0:T(1,128)}), f32[64,1,1024]{2,1,0:T(1,128)}, u32[]{:S(2)}, u32[]{:S(2)}) async-start(f32[64,1,1024]{2,1,0:T(1,128)} %reshape.1547), calls=%async_computation.3 | async-start | bytes 524288 | tf_op jit(solution)/shard_map/all_to_all | solution.py:121
  142.2 18.2 %all-to-all-done.2 = f32[64,1,1024]{2,1,0:T(1,128)} async-done(((f32[64,1,1024]{2,1,0:T(1,128)}), f32[64,1,1024]{2,1,0:T(1,128)}, u32[]{:S(2)}, u32[]{:S(2)}) %all-to-all-start.2) | async-done | bytes 262176 | tf_op jit(solution)/shard_map/all_to_all | solution.py:121
  161.0 2.2 reduce.1
  167.3 2.0 convolution_bitcast_fusion.8
  170.6 3.0 reshape.1549
  173.6 5.7 all-to-all-start.3
  180.1 5.4 all-to-all-done.3
  185.5 2.2 reduce.2
  187.8 1.9 reshape.1550
  189.6 2.8 copy.153
  192.4 1.5 all_to_all.108
  194.0 1.9 fusion.9
  197.9 2.3 reshape.1551
  200.2 10.8 %all_to_all.131 = f32[8,1,8192]{2,1,0:T(1,128)} all-to-all(f32[8,1,8192]{2,1,0:T(1,128)S(1)} %reshape.1551), channel_id=1, replica_groups=mesh['band'=8,'pw'=64] {'band'}, dimensions={0} | all-to-all | bytes 524288 | tf_op jit(solution)/shard_map/all_to_all | solution.py:127
  211.0 2.2 reduce.3
  213.2 1.9 reshape.1552
  215.1 2.8 copy.152
  220.9 1.6 copy.77
  223.6 27.7 %all_to_all.132 = f32[64,1,1024]{2,1,0:T(1,128)S(1)} all-to-all(f32[64,1,1024]{2,1,0:T(1,128)S(1)} %reshape.1553), channel_id=1, replica_groups=mesh['band'=8,'pw'=64] {'pw'}, dimensions={0} | all-to-all | bytes 524288 | tf_op jit(solution)/shard_map/all_to_all | solution.py:129
  251.2 5.4 all-to-all-start.7
  260.3 1.8 fusion.11
  262.1 8.9 %all-to-all-done.7 = s32[1,64,128]{2,0,1:T(1,128)} async-done(((s32[1,64,128]{2,0,1:T(1,128)}), s32[1,64,128]{2,0,1:T(1,128)}, u32[]{:S(2)}, u32[]{:S(2)}) %all-to-all-start.7) | async-done | bytes 32800 | tf_op jit(solution)/shard_map/all_to_all | solution.py:136
  272.1 5.2 all-to-all-start.6
  277.3 2.5 copy.57
  281.2 2.8 fusion.3
  284.0 2.3 copy.59
  286.3 5.5 all-to-all-done.6
  291.8 6.4 all-to-all-start.1
  298.3 7.0 collective-permute-start
  307.1 40.7 %collective-permute-done = f32[256,1,256]{0,2,1:T(8,128)S(1)} collective-permute-done((f32[256,1,256]{0,2,1:T(8,128)S(1)}, f32[256,1,256]{0,2,1:T(8,128)S(1)}, u32[]{:S(2)}, u32[]{:S(2)}) %collective-permute-start) | collective-permute-done | bytes 262176 | tf_op jit(solution)/shard_map/ppermute | solution.py:21
  347.9 1.9 copy.82
  349.8 1.6 reshape.1427
  351.5 45.5 %gather_fusion.7 = f32[8192]{0:T(1024)S(1)} fusion(f32[327680]{0:T(1024)S(1)} %reshape.1427, s32[8192]{0:T(1024)S(1)} %get-tuple-element.8), kind=kCustom, calls=%fused_computation.7 | custom fusion | bytes 98304 | tf_op jit(solution)/shard_map/gather | solution.py:148
  397.0 45.5 %gather_fusion.6 = f32[8192]{0:T(1024)S(1)} fusion(f32[327680]{0:T(1024)S(1)} %reshape.1427, s32[8192]{0:T(1024)S(1)} %get-tuple-element.22), kind=kCustom, calls=%fused_computation.6 | custom fusion | bytes 98304 | tf_op jit(solution)/shard_map/gather | solution.py:148
  442.5 45.5 %gather_fusion.5 = f32[8192]{0:T(1024)S(1)} fusion(f32[327680]{0:T(1024)S(1)} %reshape.1427, s32[8192]{0:T(1024)S(1)} %get-tuple-element.23), kind=kCustom, calls=%fused_computation.5 | custom fusion | bytes 98304 | tf_op jit(solution)/shard_map/gather | solution.py:148
  488.1 45.5 %gather_fusion.4 = f32[8192]{0:T(1024)S(1)} fusion(f32[327680]{0:T(1024)S(1)} %reshape.1427, s32[8192]{0:T(1024)S(1)} %get-tuple-element.24), kind=kCustom, calls=%fused_computation.4 | custom fusion | bytes 98304 | tf_op jit(solution)/shard_map/gather | solution.py:148
  533.6 45.5 %gather_fusion.3 = f32[8192]{0:T(1024)S(1)} fusion(f32[327680]{0:T(1024)S(1)} %reshape.1427, s32[8192]{0:T(1024)S(1)} %get-tuple-element.31), kind=kCustom, calls=%fused_computation.3 | custom fusion | bytes 98304 | tf_op jit(solution)/shard_map/gather | solution.py:148
  579.2 45.5 %gather_fusion.2 = f32[8192]{0:T(1024)S(1)} fusion(f32[327680]{0:T(1024)S(1)} %reshape.1427, s32[8192]{0:T(1024)S(1)} %get-tuple-element.30), kind=kCustom, calls=%fused_computation.2 | custom fusion | bytes 98304 | tf_op jit(solution)/shard_map/gather | solution.py:148
  624.7 45.5 %gather_fusion.1 = f32[8192]{0:T(1024)S(1)} fusion(f32[327680]{0:T(1024)S(1)} %reshape.1427, s32[8192]{0:T(1024)S(1)} %get-tuple-element.29), kind=kCustom, calls=%fused_computation.1 | custom fusion | bytes 98304 | tf_op jit(solution)/shard_map/gather | solution.py:148
  670.3 45.5 %gather_fusion = f32[8192]{0:T(1024)S(1)} fusion(f32[327680]{0:T(1024)S(1)} %reshape.1427, s32[8192]{0:T(1024)S(1)} %get-tuple-element.28), kind=kCustom, calls=%fused_computation | custom fusion | bytes 98304 | tf_op jit(solution)/shard_map/gather | solution.py:148
  716.9 16.1 %all-to-all-start.8 = ((f32[8,64,1,128]{3,0,2,1:T(8,128)}), f32[8,64,1,128]{3,0,2,1:T(8,128)S(1)}, u32[]{:S(2)}, u32[]{:S(2)}) async-start(f32[8,64,1,128]{3,0,2,1:T(8,128)} %stack.146), calls=%async_computation.9 | async-start | bytes 524288 | tf_op jit(solution)/shard_map/all_to_all | solution.py:150
  735.5 1.8 convolution_bitcast_fusion.2
  739.1 16.3 %all-to-all-done.8 = f32[8,64,1,128]{3,0,2,1:T(8,128)S(1)} async-done(((f32[8,64,1,128]{3,0,2,1:T(8,128)}), f32[8,64,1,128]{3,0,2,1:T(8,128)S(1)}, u32[]{:S(2)}, u32[]{:S(2)}) %all-to-all-start.8) | async-done | bytes 262176 | tf_op jit(solution)/shard_map/all_to_all | solution.py:150
  (83 shorter events, 41.5 us)
Async XLA Ops:
  7.2 1.5 copy-start.12
  11.6 74.0 %all-to-all-start = ((f32[1,2,2,256,256]{4,1,2,0,3:T(2,128)}), f32[1,2,2,256,256]{4,1,2,0,3:T(2,128)S(1)}, u32[]{:S(2)}, u32[]{:S(2)}) async-start(f32[1,2,2,256,256]{4,1,2,0,3:T(2,128)} %copy.53), calls=%async_computation | async-start | bytes 2097152 | tf_op jit(solution)/shard_map/all_to_all | solution.py:95
  30.4 87.3 %reduce-scatter.2.cloned.1.call-start = ((), (), s32[]{:S(2)}) async-start(), calls=%async_computation.10 | async-start | bytes 1179648 | tf_op jit(solution)/shard_map/reduce_scatter | solution.py:119
  91.5 26.2 %copy-start.10 = (f32[256,1,256]{2,0,1:T(8,128)}, f32[256,1,256]{2,0,1:T(8,128)S(1)}, u32[]{:S(2)}) copy-start(f32[256,1,256]{2,0,1:T(8,128)S(1)} %fusion.57) | copy-start | bytes 786436
  122.5 38.0 %all-to-all-start.2 = ((f32[64,1,1024]{2,1,0:T(1,128)}), f32[64,1,1024]{2,1,0:T(1,128)}, u32[]{:S(2)}, u32[]{:S(2)}) async-start(f32[64,1,1024]{2,1,0:T(1,128)} %reshape.1547), calls=%async_computation.3 | async-start | bytes 524288 | tf_op jit(solution)/shard_map/all_to_all | solution.py:121
  140.9 1.3 copy-start.1
  140.9 1.3 copy-start.3
  166.1 1.2 copy-start
  173.6 11.9 %all-to-all-start.3 = ((f32[8,1,8192]{2,1,0:T(1,128)}), f32[8,1,8192]{2,1,0:T(1,128)}, u32[]{:S(2)}, u32[]{:S(2)}) async-start(f32[8,1,8192]{2,1,0:T(1,128)} %reshape.1549), calls=%async_computation.4 | async-start | bytes 524288 | tf_op jit(solution)/shard_map/all_to_all | solution.py:123
  251.2 19.8 %all-to-all-start.7 = ((s32[1,64,128]{2,0,1:T(1,128)}), s32[1,64,128]{2,0,1:T(1,128)}, u32[]{:S(2)}, u32[]{:S(2)}) async-start(s32[1,64,128]{2,0,1:T(1,128)} %bitcast.301), calls=%async_computation.8 | async-start | bytes 65536 | tf_op jit(solution)/shard_map/all_to_all | solution.py:136
  259.1 1.0 copy-start.2
  259.1 1.2 copy-start.4
  272.1 19.7 %all-to-all-start.6 = ((f32[8,256,4,32]{1,3,2,0:T(8,128)}), f32[8,256,4,32]{1,3,2,0:T(8,128)S(1)}, u32[]{:S(2)}, u32[]{:S(2)}) async-start(f32[8,256,4,32]{1,3,2,0:T(8,128)} %stack.137), calls=%async_computation.7 | async-start | bytes 2097152 | tf_op jit(solution)/shard_map/all_to_all | solution.py:14
  279.9 1.4 copy-start.5
  280.4 0.7 copy-start.6
  280.4 0.8 copy-start.8
  291.8 425.1 %all-to-all-start.1 = ((f32[1,2,128,4,256]{4,1,3,0,2:T(2,128)}), f32[1,2,128,4,256]{4,1,3,0,2:T(2,128)}, u32[]{:S(2)}, u32[]{:S(2)}) async-start(f32[1,2,128,4,256]{4,1,3,0,2:T(2,128)} %copy.59), calls=%async_computation.1 | async-start | bytes 2097152 | tf_op jit(solution)/shard_map/all_to_all | solution.py:105
  298.3 49.5 %collective-permute-start = (f32[256,1,256]{0,2,1:T(8,128)S(1)}, f32[256,1,256]{0,2,1:T(8,128)S(1)}, u32[]{:S(2)}, u32[]{:S(2)}) collective-permute-start(f32[256,1,256]{0,2,1:T(8,128)S(1)} %slice.36), channel_id=1, source_target_pairs={{0,63},{1,0},{2,1},{3,2},{4,3},{5,4},{6,5},{7,6},{8,7},{9,8},{10,9... | collective-permute-start | bytes 786440 | tf_op jit(solution)/shard_map/ppermute | solution.py:21
  716.9 38.5 %all-to-all-start.8 = ((f32[8,64,1,128]{3,0,2,1:T(8,128)}), f32[8,64,1,128]{3,0,2,1:T(8,128)S(1)}, u32[]{:S(2)}, u32[]{:S(2)}) async-start(f32[8,64,1,128]{3,0,2,1:T(8,128)} %stack.146), calls=%async_computation.9 | async-start | bytes 524288 | tf_op jit(solution)/shard_map/all_to_all | solution.py:150
  734.5 1.0 copy-start.7
  734.5 1.0 copy-start.9
  737.3 18.1 %copy-start.11 = (f32[8,1,64,128]{3,2,1,0:T(8,128)S(1)}, f32[8,1,64,128]{3,2,1,0:T(8,128)}, u32[]{:S(2)}) copy-start(f32[8,1,64,128]{3,2,1,0:T(8,128)} %param.12) | copy-start | bytes 786436
  737.3 18.3 %copy-start.13 = (s32[1,64]{1,0:T(1,128)S(1)}, s32[1,64]{1,0:T(1,128)}, u32[]{:S(2)}) copy-start(s32[1,64]{1,0:T(1,128)} %param.13) | copy-start | bytes 772
Sparse Core Ops, SparseCore 0:
  89.7 27.9 reduce-scatter.1
